TPU v7x, 256 devices: a whole 4x4x8 slice. The times are simulated.
256 devices in a mesh: wide: 32 (over z, y), narrow: 8 (over x, core).
Axes of the slice: x: 4, y: 4, z: 8, core: 2. Of those that a mesh axis runs over, the one named last changes fastest.
Arguments:
- user_factors: float32 [262144, 512], P(('wide', 'narrow')), may hold values from -1.25 to 1.25
- item_factors: float32 [256, 2, 512, 512], P(('wide', 'narrow')), may hold values from -1.25 to 1.25
- tile_rows: int32 [256, 5, 2, 10], P(('wide', 'narrow')), may hold values from 0 to 7
- tile_cols: int32 [256, 5, 2, 10], P(('wide', 'narrow')), may hold values from 0 to 3
- tile_count: int32 [256, 5, 2], P(('wide', 'narrow')), may hold values from 2 to 10, as said below
- ratings: bfloat16 [256, 5, 2, 10, 128, 128], P(('wide', 'narrow')), may hold values from -6 to 6
Outputs:
- user_result: float32 [262144, 512], P(('wide', 'narrow'))
- item_result: float32 [256, 2, 512, 512], P(('wide', 'narrow'))
Inputs may be any that keep to these rules, and one draw needn't show every extreme that they name: At each visit some stratum has 10 tiles in every slot; entries of tile_rows, tile_cols and ratings at minibatch positions tile_count and beyond are not used.
All inputs are finite; a program needn't handle non-finite values.
Results may differ from a plain program's by a relative error of at most 0.0003.
Values sent between devices are 32-bit elements; how exact they have to be, the bound alone decides.
A program may use at most 64 MiB of HBM per device.

v0:
```python
import jax
import jax.numpy as jnp
from jax import lax
from jax.sharding import PartitionSpec as P

learn_rate = 0.0035
decay_weight = 0.05


def shifted(block, axis, distance):
    devices = range(lax.axis_size(axis))
    route = [((i - distance) % len(devices), i) for i in devices]
    return lax.ppermute(block, axis, route)


def tile_update(user_block, item_block, rating_tile, row_tile, col_tile):
    tile_size = rating_tile.shape[-1]
    users_part = lax.dynamic_slice_in_dim(user_block, row_tile * tile_size, tile_size, 0)
    items_part = lax.dynamic_slice_in_dim(item_block, col_tile * tile_size, tile_size, 0)
    predicted = lax.dot_general(
        users_part,
        items_part,
        (((1,), (1,)), ((), ())),
        precision=lax.Precision.HIGHEST,
        preferred_element_type=jnp.float32,
    )
    errors = predicted - rating_tile.astype(jnp.float32)
    user_grad = (
        jnp.dot(
            errors, items_part, precision=lax.Precision.HIGHEST, preferred_element_type=jnp.float32
        )
        + decay_weight * users_part
    )
    item_gradient = (
        lax.dot_general(
            errors,
            users_part,
            (((0,), (0,)), ((), ())),
            precision=lax.Precision.HIGHEST,
            preferred_element_type=jnp.float32,
        )
        + decay_weight * items_part
    )
    new_users = users_part - learn_rate * user_grad
    new_items = items_part - learn_rate * item_gradient
    user_block = lax.dynamic_update_slice_in_dim(user_block, new_users, row_tile * tile_size, 0)
    item_block = lax.dynamic_update_slice_in_dim(item_block, new_items, col_tile * tile_size, 0)
    return (user_block, item_block)


def sweep_slot(user_block, item_block, ratings_slot, rows_slot, cols_slot, tile_total):

    def one_tile(position, carried):
        user_now, item_now = carried
        return tile_update(
            user_now, item_now, ratings_slot[position], rows_slot[position], cols_slot[position]
        )

    return lax.fori_loop(0, tile_total, one_tile, (user_block, item_block))


def body(user_factors, item_factors, tile_rows, tile_cols, tile_count, ratings):
    user_block = user_factors
    held_blocks = item_factors[0]
    visits_total = ratings.shape[1]
    slot_total = ratings.shape[2]
    for visit_index in range(visits_total):
        updated = []
        for holder_position in range(slot_total):
            user_block, holder_product_factors = sweep_slot(
                user_block,
                held_blocks[holder_position],
                ratings[0, visit_index, holder_position],
                tile_rows[0, visit_index, holder_position],
                tile_cols[0, visit_index, holder_position],
                tile_count[0, visit_index, holder_position],
            )
            updated.append(holder_product_factors)
        held_blocks = jnp.stack(updated, axis=0)
        if visit_index < visits_total - 1:
            held_blocks = shifted(held_blocks, "wide", 1)
        if visit_index == visits_total - 2:
            held_blocks = shifted(held_blocks, "narrow", 1)
    return (user_block, held_blocks[None])


def solution(mesh):
    in_specs = (
        P(("wide", "narrow"), None),
        P(("wide", "narrow"), None, None, None),
        P(("wide", "narrow"), None, None, None),
        P(("wide", "narrow"), None, None, None),
        P(("wide", "narrow"), None, None),
        P(("wide", "narrow"), None, None, None, None, None),
    )
    out_specs = (P(("wide", "narrow"), None), P(("wide", "narrow"), None, None, None))
    return jax.shard_map(body, mesh=mesh, in_specs=in_specs, out_specs=out_specs, check_vma=False)
```

profile of v0, /device:TPU:134, one launch (start us, length us, event | category | flops | bytes accessed | tf_op | source)
XLA Modules:
  0.0 888.5 jit_solution(14001243721103226599)
XLA Ops:
  0.6 1.9 copy-done.2
  2.6 1.7 slice_bitcast_fusion.10
  7.4 34.7 %while.120 = (s32[]{:T(128)}, f32[1024,512]{1,0:T(8,128)S(1)}, f32[512,512]{1,0:T(8,128)}, s32[]{:T(128)}, s32[10]{0:T(128)S(1)}, /*index=5*/s32[10]{0:T(128)S(1...) while((s32[]{:T(128)}, f32[1024,512]{1,0:T(8,128)S(1)}, ...), condition=%wide.region_1.0_spmd, body=%wide.region_0.0_spmd.sunk | while | flops 302546944 | bytes 6521135 | solution.py:59
  10.5 1.3 convolution_subtract_fusion.20
  13.6 1.3 fusion.237
  19.1 1.3 convolution_subtract_fusion.20
  27.6 1.3 convolution_subtract_fusion.20
  30.6 1.3 fusion.237
  36.1 1.3 convolution_subtract_fusion.20
  39.1 1.3 fusion.237
  42.1 27.0 %while.121 = (s32[]{:T(128)}, f32[1024,512]{1,0:T(8,128)S(1)}, f32[512,512]{1,0:T(8,128)S(1)}, s32[]{:T(128)}, s32[10]{0:T(128)S(1)}, /*index=5*/s32[10]{0:T(128...) while((s32[]{:T(128)}, f32[1024,512]{1,0:T(8,128)S(1)}, ...), condition=%wide.region_3.0_spmd, body=%wide.region_2.0_spmd.sunk | while | flops 302546944 | bytes 6521135 | solution.py:59
  69.1 2.7 pad_maximum_fusion
  71.8 38.2 %collective-permute-done = f32[2,512,512]{2,1,0:T(8,128)} collective-permute-done((f32[2,512,512]{2,1,0:T(8,128)}, f32[2,512,512]{2,1,0:T(8,128)}, u32[]{:S(2)}, u32[]{:S(2)}) %collective-permute-start) | collective-permute-done | bytes 2097184 | tf_op jit(solution)/shard_map/ppermute | solution.py:13
  110.1 2.7 slice_bitcast_fusion.6
  112.8 34.5 %while.122 = (s32[]{:T(128)}, f32[1024,512]{1,0:T(8,128)S(1)}, f32[512,512]{1,0:T(8,128)}, s32[]{:T(128)}, s32[10]{0:T(128)S(1)}, /*index=5*/s32[10]{0:T(128)S(1...) while((s32[]{:T(128)}, f32[1024,512]{1,0:T(8,128)S(1)}, ...), condition=%wide.region_5.0_spmd, body=%wide.region_4.0_spmd.sunk | while | flops 302546944 | bytes 6521135 | solution.py:59
  115.9 1.3 convolution_subtract_fusion.22
  118.9 1.3 fusion.253
  124.4 1.3 convolution_subtract_fusion.22
  127.4 1.3 fusion.253
  132.8 1.3 convolution_subtract_fusion.22
  135.8 1.3 fusion.253
  141.3 1.3 convolution_subtract_fusion.22
  144.3 1.3 fusion.253
  147.3 21.7 %while.123 = (s32[]{:T(128)}, f32[1024,512]{1,0:T(8,128)S(1)}, f32[512,512]{1,0:T(8,128)S(1)}, s32[]{:T(128)}, s32[10]{0:T(128)S(1)}, /*index=5*/s32[10]{0:T(128...) while((s32[]{:T(128)}, f32[1024,512]{1,0:T(8,128)S(1)}, ...), condition=%wide.region_7.0_spmd, body=%wide.region_6.0_spmd.sunk | while | flops 302546944 | bytes 6521135 | solution.py:59
  169.0 2.7 pad_maximum_fusion.1
  171.8 203.2 %collective-permute-done.1 = f32[2,512,512]{2,1,0:T(8,128)} collective-permute-done((f32[2,512,512]{2,1,0:T(8,128)}, f32[2,512,512]{2,1,0:T(8,128)}, u32[]{:S(2)}, u32[]{:S(2)}) %collective-permute-start.1) | collective-permute-done | bytes 2097184 | tf_op jit(solution)/shard_map/ppermute | solution.py:13
  375.0 2.7 slice_bitcast_fusion.4
  377.7 17.5 %while.124 = (s32[]{:T(128)}, f32[1024,512]{1,0:T(8,128)S(1)}, f32[512,512]{1,0:T(8,128)}, s32[]{:T(128)}, s32[10]{0:T(128)S(1)}, /*index=5*/s32[10]{0:T(128)S(1...) while((s32[]{:T(128)}, f32[1024,512]{1,0:T(8,128)S(1)}, ...), condition=%wide.region_9.0_spmd, body=%wide.region_8.0_spmd.sunk | while | flops 302546944 | bytes 6521135 | solution.py:59
  380.8 1.3 convolution_subtract_fusion.24
  389.3 1.3 convolution_subtract_fusion.24
  392.3 1.3 fusion.269
  395.2 22.0 %while.125 = (s32[]{:T(128)}, f32[1024,512]{1,0:T(8,128)S(1)}, f32[512,512]{1,0:T(8,128)S(1)}, s32[]{:T(128)}, s32[10]{0:T(128)S(1)}, /*index=5*/s32[10]{0:T(128...) while((s32[]{:T(128)}, f32[1024,512]{1,0:T(8,128)S(1)}, ...), condition=%wide.region_11.0_spmd, body=%wide.region_10.0_spmd.sunk | while | flops 302546944 | bytes 6521135 | solution.py:59
  417.2 2.7 pad_maximum_fusion.2
  419.9 37.7 %collective-permute-done.2 = f32[2,512,512]{2,1,0:T(8,128)} collective-permute-done((f32[2,512,512]{2,1,0:T(8,128)}, f32[2,512,512]{2,1,0:T(8,128)}, u32[]{:S(2)}, u32[]{:S(2)}) %collective-permute-start.2) | collective-permute-done | bytes 2097184 | tf_op jit(solution)/shard_map/ppermute | solution.py:13
  457.6 2.7 slice_bitcast_fusion.2
  460.3 26.3 %while.126 = (s32[]{:T(128)}, f32[1024,512]{1,0:T(8,128)S(1)}, f32[512,512]{1,0:T(8,128)}, s32[]{:T(128)}, s32[10]{0:T(128)S(1)}, /*index=5*/s32[10]{0:T(128)S(1...) while((s32[]{:T(128)}, f32[1024,512]{1,0:T(8,128)S(1)}, ...), condition=%wide.region_13.0_spmd, body=%wide.region_12.0_spmd.sunk | while | flops 302546944 | bytes 6521135 | solution.py:59
  463.5 1.3 convolution_subtract_fusion.26
  466.5 1.3 fusion.285
  472.1 1.3 convolution_subtract_fusion.26
  480.7 1.3 convolution_subtract_fusion.26
  483.7 1.3 fusion.285
  486.6 21.5 %while.127 = (s32[]{:T(128)}, f32[1024,512]{1,0:T(8,128)S(1)}, f32[512,512]{1,0:T(8,128)S(1)}, s32[]{:T(128)}, s32[10]{0:T(128)S(1)}, /*index=5*/s32[10]{0:T(128...) while((s32[]{:T(128)}, f32[1024,512]{1,0:T(8,128)S(1)}, ...), condition=%wide.region_15.0_spmd, body=%wide.region_14.0_spmd.sunk | while | flops 302546944 | bytes 6521135 | solution.py:59
  508.1 1.4 pad_maximum_fusion.3
  510.3 28.8 %collective-permute-done.3 = f32[2,512,512]{2,1,0:T(8,128)} collective-permute-done((f32[2,512,512]{2,1,0:T(8,128)S(1)}, f32[2,512,512]{2,1,0:T(8,128)}, u32[]{:S(2)}, u32[]{:S(2)}) %collective-permute-start.3) | collective-permute-done | bytes 2097184 | tf_op jit(solution)/shard_map/ppermute | solution.py:13
  539.0 202.0 %collective-permute-done.4 = f32[2,512,512]{2,1,0:T(8,128)} collective-permute-done((f32[2,512,512]{2,1,0:T(8,128)}, f32[2,512,512]{2,1,0:T(8,128)}, u32[]{:S(2)}, u32[]{:S(2)}) %collective-permute-start.4) | collective-permute-done | bytes 2097184 | tf_op jit(solution)/shard_map/ppermute | solution.py:13
  741.0 2.7 slice_bitcast_fusion
  743.7 87.2 %while.128 = (s32[]{:T(128)}, f32[1024,512]{1,0:T(8,128)S(1)}, f32[512,512]{1,0:T(8,128)}, s32[]{:T(128)}, s32[10]{0:T(128)S(1)}, /*index=5*/s32[10]{0:T(128)S(1...) while((s32[]{:T(128)}, f32[1024,512]{1,0:T(8,128)S(1)}, ...), condition=%wide.region_17.0_spmd, body=%wide.region_16.0_spmd.sunk | while | flops 302546944 | bytes 6521135 | solution.py:59
  747.0 1.3 convolution_subtract_fusion.28
  750.1 1.3 fusion.301
  755.7 1.3 convolution_subtract_fusion.28
  758.7 1.3 fusion.301
  764.4 1.3 convolution_subtract_fusion.28
  773.0 1.3 convolution_subtract_fusion.28
  776.0 1.3 fusion.301
  781.7 1.3 convolution_subtract_fusion.28
  784.7 1.3 fusion.301
  790.3 1.3 convolution_subtract_fusion.28
  799.0 1.3 convolution_subtract_fusion.28
  802.0 1.3 fusion.301
  807.7 1.3 convolution_subtract_fusion.28
  816.3 1.3 convolution_subtract_fusion.28
  825.0 1.3 convolution_subtract_fusion.28
  830.9 54.1 %while.129 = (s32[]{:T(128)}, f32[1024,512]{1,0:T(8,128)S(1)}, f32[512,512]{1,0:T(8,128)S(1)}, s32[]{:T(128)}, s32[10]{0:T(128)S(1)}, /*index=5*/s32[10]{0:T(128...) while((s32[]{:T(128)}, f32[1024,512]{1,0:T(8,128)S(1)}, ...), condition=%wide.region_19.0_spmd, body=%wide.region_18.0_spmd.sunk | while | flops 302546944 | bytes 6521135 | solution.py:59
  885.0 3.5 maximum_bitcast_fusion
  (334 shorter events, 193.4 us)
Async XLA Ops:
  0.6 1.9 copy-start.2
  2.6 1.7 copy-start.4
  2.6 2.4 copy-start.5
  2.6 2.4 copy-start.6
  2.6 2.8 copy-start.3
  5.4 2.0 copy-start.1
  71.8 38.2 %collective-permute-start = (f32[2,512,512]{2,1,0:T(8,128)}, f32[2,512,512]{2,1,0:T(8,128)}, u32[]{:S(2)}, u32[]{:S(2)}) collective-permute-start(f32[2,512,512]{2,1,0:T(8,128)} %pad_maximum_fusion), channel_id=1, source_target_pairs={{248,0},{0,8},{8,16},{16,24},{24,32},{32,40},{40,48},{48,56},{56,6... | collective-permute-start | bytes 6291464 | tf_op jit(solution)/shard_map/ppermute | solution.py:13
  171.8 203.3 %collective-permute-start.1 = (f32[2,512,512]{2,1,0:T(8,128)}, f32[2,512,512]{2,1,0:T(8,128)}, u32[]{:S(2)}, u32[]{:S(2)}) collective-permute-start(f32[2,512,512]{2,1,0:T(8,128)} %pad_maximum_fusion.1), channel_id=1, source_target_pairs={{248,0},{0,8},{8,16},{16,24},{24,32},{32,40},{40,48},{48,56},{56,6... | collective-permute-start | bytes 6291464 | tf_op jit(solution)/shard_map/ppermute | solution.py:13
  419.9 37.7 %collective-permute-start.2 = (f32[2,512,512]{2,1,0:T(8,128)}, f32[2,512,512]{2,1,0:T(8,128)}, u32[]{:S(2)}, u32[]{:S(2)}) collective-permute-start(f32[2,512,512]{2,1,0:T(8,128)} %pad_maximum_fusion.2), channel_id=1, source_target_pairs={{248,0},{0,8},{8,16},{16,24},{24,32},{32,40},{40,48},{48,56},{56,6... | collective-permute-start | bytes 6291464 | tf_op jit(solution)/shard_map/ppermute | solution.py:13
  509.5 29.5 %collective-permute-start.3 = (f32[2,512,512]{2,1,0:T(8,128)S(1)}, f32[2,512,512]{2,1,0:T(8,128)}, u32[]{:S(2)}, u32[]{:S(2)}) collective-permute-start(f32[2,512,512]{2,1,0:T(8,128)S(1)} %pad_maximum_fusion.3), channel_id=1, source_target_pairs={{248,0},{0,8},{8,16},{16,24},{24,32},{32,40},{40,48},{48,56},{56,6... | collective-permute-start | bytes 6291464 | tf_op jit(solution)/shard_map/ppermute | solution.py:13
  539.0 202.0 %collective-permute-start.4 = (f32[2,512,512]{2,1,0:T(8,128)}, f32[2,512,512]{2,1,0:T(8,128)}, u32[]{:S(2)}, u32[]{:S(2)}) collective-permute-start(f32[2,512,512]{2,1,0:T(8,128)} %collective-permute-done.3), channel_id=1, source_target_pairs={{7,0},{0,1},{1,2},{2,3},{3,4},{4,5},{5,6},{6,7},{15,8},{8,9},{9,10... | collective-permute-start | bytes 6291464 | tf_op jit(solution)/shard_map/ppermute | solution.py:13
  885.0 3.5 copy-start
where the time goes:
time: 897 us; the launch traced here: 888 us
  waiting for transfers between devices  510 us (57%)
  local copies, waits for them, and re-layouts  133 us (15%)
  matrix products  124 us (14%)
  loops' own time  106 us (12%)
  other arithmetic  13 us (1%)
    ppermute x5, waiting for transfers between devices, shifted(): return lax.ppermute(block, axis, route)  510 us
    another operation x10, loops' own time, sweep_slot(): return lax.fori_loop(0, tile_total, one_tile, (user_block, item_block))  106 us
    dot_general x50, matrix products, tile_update(): lax.dot_general(users_part, items_part, (((1,), (1,)), ((), ())), precisi...  61.7 us
    while x100, local copies, waits for them, and re-layouts  54.5 us
    dot_general x50, matrix products, tile_update(): jnp.dot(errors, items_part, precision=lax.Precision.HIGHEST, preferred_el...  41.1 us
    dynamic_slice x50, local copies, waits for them, and re-layouts, one_tile(): cols_slot[position]  30.8 us
    dynamic_slice x50, local copies, waits for them, and re-layouts, one_tile(): rows_slot[position]  30.7 us
    dot_general x50, matrix products, tile_update(): lax.dot_general(errors, users_part, (((0,), (0,)), ((), ())), precision=l...  21.7 us
  transfers between devices with their start and end apart: 5, of which 5 were waited for; matrix products, arithmetic and copies ran while one was open for 0% of the time, Pallas kernels for 0%

commit v1 on v0

v1 whole, which is shorter than its diff:
```python
import functools

import jax
import jax.numpy as jnp
from jax import lax
from jax.experimental import pallas as pl
from jax.experimental.pallas import tpu as pltpu
from jax.sharding import PartitionSpec as P

learn_rate = 0.0035
decay_weight = 0.05

RING = 4
TILE = 128
RELAY_ROWS = 112
MESH = pl.DeviceIdType.MESH


def split(x):
    high = x.astype(jnp.bfloat16)
    return high, (x - high.astype(jnp.float32)).astype(jnp.bfloat16)


def tile_update(users, items, rating):
    uh, ul = split(users)
    ih, il = split(items)
    s = lax.dot_general(
        jnp.concatenate([uh, ul], 0),
        jnp.concatenate([ih, il], 0),
        (((1,), (1,)), ((), ())),
        preferred_element_type=jnp.float32,
    )
    t = TILE
    errors = (s[:t, :t] + (s[:t, t:] + s[t:, :t])) - rating.astype(jnp.float32)
    eh, el = split(errors)
    user_grad = jnp.dot(
        jnp.concatenate([eh, el, eh], 1),
        jnp.concatenate([ih, ih, il], 0),
        preferred_element_type=jnp.float32,
    )
    th, tl = split(errors.T)
    item_grad = jnp.dot(
        jnp.concatenate([th, tl, th], 1),
        jnp.concatenate([uh, uh, ul], 0),
        preferred_element_type=jnp.float32,
    )
    new_users = users - learn_rate * (user_grad + decay_weight * users)
    new_items = items - learn_rate * (item_grad + decay_weight * items)
    return new_users, new_items


def pick(values, index):
    out = values[0]
    for i in range(1, len(values)):
        out = jnp.where(index == i, values[i], out)
    return out


def kernel(
    n_wide,
    n_narrow,
    visits,
    slots,
    most,
    users_ref,
    items_ref,
    ratings_ref,
    rows_ref,
    cols_ref,
    count_ref,
    users_out,
    items_out,
    users,
    work,
    held,
    relay_one,
    relay_two,
    ratings,
    load_sem,
    rating_sem,
    send_sem,
    recv_sem,
):
    steps = visits * slots
    moves = steps - slots
    user_tiles = users_ref.shape[0]
    block_rows = items_ref.shape[2]
    item_tiles = block_rows // TILE
    straight = block_rows - RELAY_ROWS

    w = lax.axis_index("wide")
    n = lax.axis_index("narrow")
    y = lax.rem(w, RING)
    base = w - y
    after = lax.rem(w + 1, n_wide)
    before = lax.rem(w + n_wide - 1, n_wide)
    down = base + lax.rem(y + RING - 1, RING)
    up = base + lax.rem(y + 1, RING)
    third_to = lax.rem(down + jnp.where(y == RING - 3, RING, 0), n_wide)
    third_from = lax.rem(up + n_wide - jnp.where(y == 0, RING, 0), n_wide)
    n_after = lax.rem(n + 1, n_narrow)
    n_before = lax.rem(n + n_narrow - 1, n_narrow)

    loads = [
        pltpu.make_async_copy(items_ref.at[0, 0], held.at[0], load_sem.at[0]),
        pltpu.make_async_copy(users_ref, users.at[pl.ds(0, user_tiles)], load_sem.at[2]),
        pltpu.make_async_copy(items_ref.at[0, 1], held.at[1], load_sem.at[1]),
    ]

    def rating_copy(t):
        return pltpu.make_async_copy(
            ratings_ref.at[0, t // slots, lax.rem(t, slots)], ratings.at[t], rating_sem.at[t]
        )

    loads[0].start()
    loads[1].start()
    rating_copy(0).start()
    loads[2].start()
    for t in range(1, steps):
        rating_copy(t).start()

    barrier = pltpu.get_barrier_semaphore()
    partners = [
        (after, n),
        (before, n),
        (down, n),
        (up, n),
        (third_to, n),
        (third_from, n),
        (after, n_after),
        (before, n_before),
        (third_to, n_after),
        (third_from, n_before),
    ]
    for partner in partners:
        pl.semaphore_signal(barrier, inc=1, device_id=partner, device_id_type=MESH)
    pl.semaphore_wait(barrier, len(partners))

    def remote(kind, t, src, dst, device):
        return pltpu.make_async_remote_copy(
            src_ref=src,
            dst_ref=dst,
            send_sem=send_sem.at[kind, t],
            recv_sem=recv_sem.at[kind, t],
            device_id=device,
            device_id_type=MESH,
        )

    def ending_n(t):
        return jnp.where(t >= moves - slots, n_after, n)

    def direct(t):
        rows = pl.ds(0, straight)
        return remote(0, t, held.at[t, rows], held.at[t + slots, rows], (after, ending_n(t)))

    def hop_one(t):
        return remote(1, t, held.at[t, pl.ds(straight, RELAY_ROWS)], relay_one.at[t], (down, n))

    def hop_two(t):
        return remote(2, t, relay_one.at[t], relay_two.at[t], (down, n))

    def hop_three(t):
        rows = pl.ds(straight, RELAY_ROWS)
        return remote(3, t, relay_two.at[t], held.at[t + slots, rows], (third_to, ending_n(t)))

    loads[0].wait()
    loads[1].wait()

    def step(t, carry):
        visit, slot = t // slots, lax.rem(t, slots)
        count = count_ref[0, visit, slot]

        @pl.when(t == 1)
        def _():
            loads[2].wait()

        rating_copy(t).wait()

        @pl.when(t >= slots)
        def _():
            direct(t - slots).wait_recv()
            hop_three(t - slots).wait_recv()

        for i in range(item_tiles):
            work[i] = held[t, i * TILE : (i + 1) * TILE, :]

        def one(k, state):
            user_at, item_at = state
            live = k < count
            a = jnp.where(live, rows_ref[0, visit, slot, k], 0)
            c = jnp.where(live, cols_ref[0, visit, slot, k], 0)
            ua = pick(user_at, a)
            ia = pick(item_at, c)
            new_users, new_items = tile_update(
                users[ua],
                work[ia],
                ratings[t, k],
            )
            users[user_tiles + k] = new_users
            work[item_tiles + k] = new_items
            user_at = tuple(
                jnp.where(live & (a == i), user_tiles + k, v) for i, v in enumerate(user_at)
            )
            item_at = tuple(
                jnp.where(live & (c == i), item_tiles + k, v) for i, v in enumerate(item_at)
            )
            return user_at, item_at

        state = (
            tuple(jnp.int32(i) for i in range(user_tiles)),
            tuple(jnp.int32(i) for i in range(item_tiles)),
        )
        state = lax.fori_loop(0, most // 2, one, state)

        @pl.when((t >= 1) & (t <= moves))
        def _():
            hop_one(t - 1).wait_recv()
            hop_two(t - 1).start()

        user_at, item_at = lax.fori_loop(most // 2, most, one, state)

        for i in range(item_tiles):
            held[t, i * TILE : (i + 1) * TILE, :] = work[item_at[i]]

        @pl.when(t < moves)
        def _():
            hop_one(t).start()
            direct(t).start()

        for i in range(user_tiles):
            users[i] = users[user_at[i]]

        @pl.when((t >= 1) & (t <= moves))
        def _():
            hop_two(t - 1).wait_recv()
            hop_three(t - 1).start()

        return carry

    lax.fori_loop(0, steps, step, 0)

    stores = [
        pltpu.make_async_copy(users.at[pl.ds(0, user_tiles)], users_out, load_sem.at[2])
    ]
    for s in range(slots):
        stores.append(
            pltpu.make_async_copy(held.at[moves + s], items_out.at[0, s], load_sem.at[s])
        )
    for copy in stores:
        copy.start()

    def drain(t, carry):
        for make in (direct, hop_one, hop_two, hop_three):
            make(t).wait_send()
        return carry

    lax.fori_loop(0, moves, drain, 0)
    for copy in stores:
        copy.wait()


def body(n_wide, n_narrow, user_factors, item_factors, tile_rows, tile_cols, tile_count, ratings):
    visits, slots, most = tile_rows.shape[1:]
    steps = visits * slots
    moves = steps - slots
    rank = user_factors.shape[1]
    user_tiles = user_factors.shape[0] // TILE
    user_blocks = user_factors.reshape(user_tiles, TILE, rank)
    block_rows = item_factors.shape[2]
    anywhere = pl.BlockSpec(memory_space=pl.ANY)
    smem = pl.BlockSpec(memory_space=pltpu.SMEM)
    f32 = jnp.float32
    users_new, items_new = pl.pallas_call(
        functools.partial(kernel, n_wide, n_narrow, visits, slots, most),
        out_shape=(
            jax.ShapeDtypeStruct(user_blocks.shape, f32),
            jax.ShapeDtypeStruct(item_factors.shape, f32),
        ),
        in_specs=[anywhere, anywhere, anywhere, smem, smem, smem],
        out_specs=(anywhere, anywhere),
        scratch_shapes=[
            pltpu.VMEM((user_tiles + most, TILE, rank), f32),
            pltpu.VMEM((block_rows // TILE + most, TILE, rank), f32),
            pltpu.VMEM((steps, block_rows, rank), f32),
            pltpu.VMEM((moves, RELAY_ROWS, rank), f32),
            pltpu.VMEM((moves, RELAY_ROWS, rank), f32),
            pltpu.VMEM((steps, most, TILE, TILE), ratings.dtype),
            pltpu.SemaphoreType.DMA((3,)),
            pltpu.SemaphoreType.DMA((steps,)),
            pltpu.SemaphoreType.DMA((4, moves)),
            pltpu.SemaphoreType.DMA((4, moves)),
        ],
        compiler_params=pltpu.CompilerParams(
            collective_id=0, has_side_effects=True, vmem_limit_bytes=40 << 20
        ),
        name="sgd_sweep",
    )(user_blocks, item_factors, ratings, tile_rows, tile_cols, tile_count)
    return users_new.reshape(user_factors.shape), items_new


def solution(mesh):
    both = ("wide", "narrow")
    in_specs = (
        P(both, None),
        P(both, None, None, None),
        P(both, None, None, None),
        P(both, None, None, None),
        P(both, None, None),
        P(both, None, None, None, None, None),
    )
    out_specs = (P(both, None), P(both, None, None, None))
    run = functools.partial(body, mesh.shape["wide"], mesh.shape["narrow"])
    return jax.shard_map(run, mesh=mesh, in_specs=in_specs, out_specs=out_specs, check_vma=False)
```

time: 897 us -> 195 us (0.22)
  the two profiles are of different devices: /device:TPU:134 before, /device:TPU:8 now
where the time goes in v1:
time: 195 us
  Pallas kernels  185 us (95%)
  local copies, waits for them, and re-layouts  9.89 us (5%)
    pallas_call x1, Pallas kernels, body(): pl.pallas_call(functools.partial(kernel, n_wide, n_narrow, visits, slots,...  185 us
    unnamed x13, local copies, waits for them, and re-layouts  9.89 us

profile of v1, /device:TPU:8, one launch (start us, length us, event | category | flops | bytes accessed | tf_op | source)
XLA Modules:
  0.0 195.1 jit_solution(17832805068666840994)
XLA Ops:
  0.6 0.8 copy.8.count_ref
  1.4 0.0 copy-start
  1.4 1.9 copy-done
  3.3 0.0 copy-start.1
  3.3 1.6 copy-done.1
  4.9 0.0 copy-start.2
  4.9 1.6 copy-done.2
  6.5 0.0 copy-start.3
  6.5 0.7 copy-done.3
  7.2 0.0 copy-start.4
  7.2 0.7 copy-done.4
  7.9 184.6 %sgd_sweep.1 = (f32[8,128,512]{2,1,0:T(8,128)S(1)}, f32[1,2,512,512]{3,2,1,0:T(8,128)S(1)}) custom-call(f32[8,128,512]{2,1,0:T(8,128)S(1)} %bitcast.2, f32[1,2,512,512]{3,2,1,0:T(8,128)S(1)} %copy-done.2, bf16[1,5,2,10,128,128]{5,4,3,2,1,0:T(8,128)(2,1)S(1)} %copy-done, s32[1,5,2,10]{3,2,1,0:T(2,128)S(1)} %copy-done.3, s32[1,5,2,10]{3,2,1,0:T(2,128)S(1)} %copy-done.4, ...), custom_call_target="tpu_custom_call" | custom-call | tf_op jit(solution)/shard_map/sgd_sweep/pallas_call | solution.py:273
  192.5 1.3 copy.11
  193.8 1.3 copy.12
Async XLA Ops:
  1.4 1.9 copy-start
  3.3 1.6 copy-start.1
  4.9 1.6 copy-start.2
  6.5 0.7 copy-start.3
  7.2 0.7 copy-start.4

commit v2 on v1

--- a/solution.py
+++ b/solution.py
@@ -12,7 +12,10 @@
 
 RING = 4
 TILE = 128
-RELAY_ROWS = 112
+RELAY_ROWS = 128
+CHUNKS = 2
+CHUNK_ROWS = RELAY_ROWS // CHUNKS
+FORWARDS = ((0, 2, 0), (2, 2, 1), (4, 3, 0), (8, 3, 1))
 MESH = pl.DeviceIdType.MESH
 
 
@@ -21,32 +24,35 @@
     return high, (x - high.astype(jnp.float32)).astype(jnp.bfloat16)
 
 
+def step_of(products, rating):
+    t = TILE
+    errors = (products[:t, :t] + (products[:t, t:] + products[t:, :t])) - rating
+    return errors * -learn_rate
+
+
 def tile_update(users, items, rating):
     uh, ul = split(users)
     ih, il = split(items)
-    s = lax.dot_general(
-        jnp.concatenate([uh, ul], 0),
-        jnp.concatenate([ih, il], 0),
-        (((1,), (1,)), ((), ())),
-        preferred_element_type=jnp.float32,
-    )
-    t = TILE
-    errors = (s[:t, :t] + (s[:t, t:] + s[t:, :t])) - rating.astype(jnp.float32)
-    eh, el = split(errors)
-    user_grad = jnp.dot(
+    rating = rating.astype(jnp.float32)
+    u_both, i_both = jnp.concatenate([uh, ul], 0), jnp.concatenate([ih, il], 0)
+    rows_by_rows = (((1,), (1,)), ((), ()))
+    f32 = jnp.float32
+    s = lax.dot_general(u_both, i_both, rows_by_rows, preferred_element_type=f32)
+    s_turned = lax.dot_general(i_both, u_both, rows_by_rows, preferred_element_type=f32)
+    eh, el = split(step_of(s, rating))
+    th, tl = split(step_of(s_turned, rating.T))
+    user_step = jnp.dot(
         jnp.concatenate([eh, el, eh], 1),
         jnp.concatenate([ih, ih, il], 0),
-        preferred_element_type=jnp.float32,
+        preferred_element_type=f32,
     )
-    th, tl = split(errors.T)
-    item_grad = jnp.dot(
+    item_step = jnp.dot(
         jnp.concatenate([th, tl, th], 1),
         jnp.concatenate([uh, uh, ul], 0),
-        preferred_element_type=jnp.float32,
+        preferred_element_type=f32,
     )
-    new_users = users - learn_rate * (user_grad + decay_weight * users)
-    new_items = items - learn_rate * (item_grad + decay_weight * items)
-    return new_users, new_items
+    keep = 1.0 - learn_rate * decay_weight
+    return users * keep + user_step, items * keep + item_step
 
 
 def pick(values, index):
@@ -115,10 +121,6 @@
     loads[0].start()
     loads[1].start()
     rating_copy(0).start()
-    loads[2].start()
-    for t in range(1, steps):
-        rating_copy(t).start()
-
     barrier = pltpu.get_barrier_semaphore()
     partners = [
         (after, n),
@@ -153,22 +155,27 @@
         rows = pl.ds(0, straight)
         return remote(0, t, held.at[t, rows], held.at[t + slots, rows], (after, ending_n(t)))
 
-    def hop_one(t):
-        return remote(1, t, held.at[t, pl.ds(straight, RELAY_ROWS)], relay_one.at[t], (down, n))
-
-    def hop_two(t):
-        return remote(2, t, relay_one.at[t], relay_two.at[t], (down, n))
-
-    def hop_three(t):
-        rows = pl.ds(straight, RELAY_ROWS)
-        return remote(3, t, relay_two.at[t], held.at[t + slots, rows], (third_to, ending_n(t)))
+    def hop(number, chunk, t):
+        kind = 1 + (number - 1) * CHUNKS + chunk
+        rows = pl.ds(straight + chunk * CHUNK_ROWS, CHUNK_ROWS)
+        if number == 1:
+            src, dst, device = held.at[t, rows], relay_one.at[t, chunk], (down, n)
+        elif number == 2:
+            src, dst, device = relay_one.at[t, chunk], relay_two.at[t, chunk], (down, n)
+        else:
+            src, dst = relay_two.at[t, chunk], held.at[t + slots, rows]
+            device = (third_to, ending_n(t))
+        return remote(kind, t, src, dst, device)
 
     loads[0].wait()
     loads[1].wait()
+    loads[2].start()
+    for t in range(1, steps):
+        rating_copy(t).start()
 
     def step(t, carry):
         visit, slot = t // slots, lax.rem(t, slots)
-        count = count_ref[0, visit, slot]
+        count = count_ref[0, slot, visit]
 
         @pl.when(t == 1)
         def _():
@@ -179,7 +186,8 @@
         @pl.when(t >= slots)
         def _():
             direct(t - slots).wait_recv()
-            hop_three(t - slots).wait_recv()
+            for chunk in range(CHUNKS):
+                hop(3, chunk, t - slots).wait_recv()
 
         for i in range(item_tiles):
             work[i] = held[t, i * TILE : (i + 1) * TILE, :]
@@ -210,30 +218,32 @@
             tuple(jnp.int32(i) for i in range(user_tiles)),
             tuple(jnp.int32(i) for i in range(item_tiles)),
         )
-        state = lax.fori_loop(0, most // 2, one, state)
-
-        @pl.when((t >= 1) & (t <= moves))
-        def _():
-            hop_one(t - 1).wait_recv()
-            hop_two(t - 1).start()
-
-        user_at, item_at = lax.fori_loop(most // 2, most, one, state)
+        done = 0
+        for position, number, chunk in FORWARDS:
+            if position > done:
+                state = lax.fori_loop(done, position, one, state, unroll=2)
+                done = position
+
+            @pl.when((t >= 1) & (t <= moves))
+            def _():
+                hop(number - 1, chunk, t - 1).wait_recv()
+                hop(number, chunk, t - 1).start()
+
+        if done < most:
+            state = lax.fori_loop(done, most, one, state, unroll=2)
+        user_at, item_at = state
 
         for i in range(item_tiles):
             held[t, i * TILE : (i + 1) * TILE, :] = work[item_at[i]]
 
         @pl.when(t < moves)
         def _():
-            hop_one(t).start()
+            for chunk in range(CHUNKS):
+                hop(1, chunk, t).start()
             direct(t).start()
 
         for i in range(user_tiles):
             users[i] = users[user_at[i]]
-
-        @pl.when((t >= 1) & (t <= moves))
-        def _():
-            hop_two(t - 1).wait_recv()
-            hop_three(t - 1).start()
 
         return carry
 
@@ -250,8 +260,10 @@
         copy.start()
 
     def drain(t, carry):
-        for make in (direct, hop_one, hop_two, hop_three):
-            make(t).wait_send()
+        direct(t).wait_send()
+        for number in (1, 2, 3):
+            for chunk in range(CHUNKS):
+                hop(number, chunk, t).wait_send()
         return carry
 
     lax.fori_loop(0, moves, drain, 0)
@@ -268,6 +280,7 @@
     user_blocks = user_factors.reshape(user_tiles, TILE, rank)
     block_rows = item_factors.shape[2]
     anywhere = pl.BlockSpec(memory_space=pl.ANY)
+    hbm = pl.BlockSpec(memory_space=pltpu.HBM)
     smem = pl.BlockSpec(memory_space=pltpu.SMEM)
     f32 = jnp.float32
     users_new, items_new = pl.pallas_call(
@@ -276,25 +289,25 @@
             jax.ShapeDtypeStruct(user_blocks.shape, f32),
             jax.ShapeDtypeStruct(item_factors.shape, f32),
         ),
-        in_specs=[anywhere, anywhere, anywhere, smem, smem, smem],
+        in_specs=[hbm, hbm, hbm, smem, smem, smem],
         out_specs=(anywhere, anywhere),
         scratch_shapes=[
             pltpu.VMEM((user_tiles + most, TILE, rank), f32),
             pltpu.VMEM((block_rows // TILE + most, TILE, rank), f32),
             pltpu.VMEM((steps, block_rows, rank), f32),
-            pltpu.VMEM((moves, RELAY_ROWS, rank), f32),
-            pltpu.VMEM((moves, RELAY_ROWS, rank), f32),
+            pltpu.VMEM((moves, CHUNKS, CHUNK_ROWS, rank), f32),
+            pltpu.VMEM((moves, CHUNKS, CHUNK_ROWS, rank), f32),
             pltpu.VMEM((steps, most, TILE, TILE), ratings.dtype),
             pltpu.SemaphoreType.DMA((3,)),
             pltpu.SemaphoreType.DMA((steps,)),
-            pltpu.SemaphoreType.DMA((4, moves)),
-            pltpu.SemaphoreType.DMA((4, moves)),
+            pltpu.SemaphoreType.DMA((1 + 3 * CHUNKS, moves)),
+            pltpu.SemaphoreType.DMA((1 + 3 * CHUNKS, moves)),
         ],
         compiler_params=pltpu.CompilerParams(
-            collective_id=0, has_side_effects=True, vmem_limit_bytes=40 << 20
+            collective_id=0, has_side_effects=True, vmem_limit_bytes=56 << 20
         ),
         name="sgd_sweep",
-    )(user_blocks, item_factors, ratings, tile_rows, tile_cols, tile_count)
+    )(user_blocks, item_factors, ratings, tile_rows, tile_cols, tile_count.swapaxes(1, 2))
     return users_new.reshape(user_factors.shape), items_new
 
 

time: 195 us -> 176 us (0.903)
  the two profiles are of different devices: /device:TPU:8 before, /device:TPU:15 now
where the time goes in v2:
time: 176 us
  Pallas kernels  171 us (97%)
  local copies, waits for them, and re-layouts  4.55 us (3%)
    pallas_call x1, Pallas kernels, body(): pl.pallas_call(functools.partial(kernel, n_wide, n_narrow, visits, slots,...  171 us
    unnamed x4, local copies, waits for them, and re-layouts  4.55 us

profile of v2, /device:TPU:15, one launch (start us, length us, event | category | flops | bytes accessed | tf_op | source)
XLA Modules:
  0.0 176.0 jit_solution(11891326681328355377)
XLA Ops:
  0.6 170.8 %sgd_sweep.1 = (f32[8,128,512]{2,1,0:T(8,128)}, f32[1,2,512,512]{3,2,1,0:T(8,128)}) custom-call(f32[8,128,512]{2,1,0:T(8,128)} %bitcast.4, f32[1,2,512,512]{3,2,1,0:T(8,128)} %items_ref.1, bf16[1,5,2,10,128,128]{5,4,3,2,1,0:T(8,128)(2,1)} %ratings_ref.1, s32[1,5,2,10]{3,2,1,0:T(2,128)} %rows_ref.1, s32[1,5,2,10]{3,2,1,0:T(2,128)} %cols_ref.1, s32[1,2,5]{2,1,0:T(2,128)} %bitcast.5), custom_call_target="tpu_custom_call" | custom-call | tf_op jit(solution)/shard_map/sgd_sweep/pallas_call | solution.py:286
  171.4 0.0 copy-start
  171.4 3.2 %copy.10 = f32[1024,512]{1,0:T(8,128)} copy(f32[1024,512]{1,0:T(8,128)} %bitcast.3) | data formatting | bytes 4194304
  174.7 0.0 copy-done
  174.7 1.3 copy.11
Async XLA Ops:
  171.4 3.2 %copy-start = (f32[1,2,512,512]{3,2,1,0:T(8,128)S(1)}, f32[1,2,512,512]{3,2,1,0:T(8,128)}, u32[]{:S(2)}) copy-start(f32[1,2,512,512]{3,2,1,0:T(8,128)} %get-tuple-element.9) | copy-start | bytes 6291460

commit v3 on v2

--- a/solution.py
+++ b/solution.py
@@ -13,6 +13,7 @@
 RING = 4
 TILE = 128
 RELAY_ROWS = 128
+VMEM_GRANT = 56 << 20
 CHUNKS = 2
 CHUNK_ROWS = RELAY_ROWS // CHUNKS
 FORWARDS = ((0, 2, 0), (2, 2, 1), (4, 3, 0), (8, 3, 1))
@@ -75,7 +76,7 @@
     cols_ref,
     count_ref,
     users_out,
-    items_out,
+    blocks_out,
     users,
     work,
     held,
@@ -170,7 +171,7 @@
     loads[0].wait()
     loads[1].wait()
     loads[2].start()
-    for t in range(1, steps):
+    for t in range(1, moves + 1):
         rating_copy(t).start()
 
     def step(t, carry):
@@ -247,17 +248,20 @@
 
         return carry
 
-    lax.fori_loop(0, steps, step, 0)
+    lax.fori_loop(0, moves + 1, step, 0)
 
     stores = [
-        pltpu.make_async_copy(users.at[pl.ds(0, user_tiles)], users_out, load_sem.at[2])
+        pltpu.make_async_copy(users.at[pl.ds(0, user_tiles)], users_out, load_sem.at[2]),
+        pltpu.make_async_copy(held.at[moves], blocks_out.at[0], load_sem.at[0]),
     ]
-    for s in range(slots):
-        stores.append(
-            pltpu.make_async_copy(held.at[moves + s], items_out.at[0, s], load_sem.at[s])
-        )
     for copy in stores:
         copy.start()
+
+    direct(moves - 1).wait_recv()
+    for chunk in range(CHUNKS):
+        hop(3, chunk, moves - 1).wait_recv()
+    last = pltpu.make_async_copy(held.at[moves + 1], blocks_out.at[1], load_sem.at[1])
+    last.start()
 
     def drain(t, carry):
         direct(t).wait_send()
@@ -269,6 +273,48 @@
     lax.fori_loop(0, moves, drain, 0)
     for copy in stores:
         copy.wait()
+    last.wait()
+
+
+def last_kernel(
+    visit,
+    slot,
+    users_ref,
+    blocks_ref,
+    ratings_ref,
+    rows_ref,
+    cols_ref,
+    count_ref,
+    users_out,
+    items_out,
+    users,
+    items,
+    ratings,
+    sems,
+):
+    users_in = pltpu.make_async_copy(users_ref, users, sems.at[0])
+    items_in = pltpu.make_async_copy(blocks_ref.at[slot], items, sems.at[1])
+    ratings_in = pltpu.make_async_copy(ratings_ref.at[0, visit, slot], ratings, sems.at[2])
+    rest = pltpu.make_async_copy(blocks_ref.at[0], items_out.at[0, 0], sems.at[3])
+    for copy in (users_in, items_in, ratings_in, rest):
+        copy.start()
+    for copy in (users_in, items_in, ratings_in):
+        copy.wait()
+
+    def one(k, carry):
+        a, c = rows_ref[0, visit, slot, k], cols_ref[0, visit, slot, k]
+        users[a], items[c] = tile_update(users[a], items[c], ratings[k])
+        return carry
+
+    lax.fori_loop(0, count_ref[0, slot, visit], one, 0)
+
+    users_back = pltpu.make_async_copy(users, users_out, sems.at[0])
+    items_back = pltpu.make_async_copy(items, items_out.at[0, slot], sems.at[1])
+    users_back.start()
+    items_back.start()
+    rest.wait()
+    users_back.wait()
+    items_back.wait()
 
 
 def body(n_wide, n_narrow, user_factors, item_factors, tile_rows, tile_cols, tile_count, ratings):
@@ -283,11 +329,13 @@
     hbm = pl.BlockSpec(memory_space=pltpu.HBM)
     smem = pl.BlockSpec(memory_space=pltpu.SMEM)
     f32 = jnp.float32
-    users_new, items_new = pl.pallas_call(
+    tables = (tile_rows, tile_cols, tile_count.swapaxes(1, 2))
+    shape = jax.ShapeDtypeStruct
+    users_then, blocks_then = pl.pallas_call(
         functools.partial(kernel, n_wide, n_narrow, visits, slots, most),
         out_shape=(
-            jax.ShapeDtypeStruct(user_blocks.shape, f32),
-            jax.ShapeDtypeStruct(item_factors.shape, f32),
+            shape(user_blocks.shape, f32),
+            shape(item_factors.shape[1:], f32),
         ),
         in_specs=[hbm, hbm, hbm, smem, smem, smem],
         out_specs=(anywhere, anywhere),
@@ -297,18 +345,36 @@
             pltpu.VMEM((steps, block_rows, rank), f32),
             pltpu.VMEM((moves, CHUNKS, CHUNK_ROWS, rank), f32),
             pltpu.VMEM((moves, CHUNKS, CHUNK_ROWS, rank), f32),
-            pltpu.VMEM((steps, most, TILE, TILE), ratings.dtype),
+            pltpu.VMEM((moves + 1, most, TILE, TILE), ratings.dtype),
             pltpu.SemaphoreType.DMA((3,)),
-            pltpu.SemaphoreType.DMA((steps,)),
+            pltpu.SemaphoreType.DMA((moves + 1,)),
             pltpu.SemaphoreType.DMA((1 + 3 * CHUNKS, moves)),
             pltpu.SemaphoreType.DMA((1 + 3 * CHUNKS, moves)),
         ],
         compiler_params=pltpu.CompilerParams(
-            collective_id=0, has_side_effects=True, vmem_limit_bytes=56 << 20
+            collective_id=0, has_side_effects=True, vmem_limit_bytes=VMEM_GRANT
         ),
         name="sgd_sweep",
-    )(user_blocks, item_factors, ratings, tile_rows, tile_cols, tile_count.swapaxes(1, 2))
-    return users_new.reshape(user_factors.shape), items_new
+    )(user_blocks, item_factors, ratings, *tables)
+    item_tiles = block_rows // TILE
+    users_new, items_new = pl.pallas_call(
+        functools.partial(last_kernel, visits - 1, slots - 1),
+        out_shape=(
+            shape(user_blocks.shape, f32),
+            shape((1, slots, item_tiles, TILE, rank), f32),
+        ),
+        in_specs=[anywhere, anywhere, hbm, smem, smem, smem],
+        out_specs=(anywhere, anywhere),
+        scratch_shapes=[
+            pltpu.VMEM(user_blocks.shape, f32),
+            pltpu.VMEM((item_tiles, TILE, rank), f32),
+            pltpu.VMEM((most, TILE, TILE), ratings.dtype),
+            pltpu.SemaphoreType.DMA((4,)),
+        ],
+        compiler_params=pltpu.CompilerParams(vmem_limit_bytes=VMEM_GRANT),
+        name="last_slot",
+    )(users_then, blocks_then.reshape(slots, item_tiles, TILE, rank), ratings, *tables)
+    return users_new.reshape(user_factors.shape), items_new.reshape(item_factors.shape)
 
 
 def solution(mesh):

time: 176 us -> 198 us (1.12)
  Pallas kernels: 171 us -> 196 us
  local copies, waits for them, and re-layouts: 4.55 us -> 0 us
    pallas_call x0 -> x1, Pallas kernels: none -> 33.8 us  [body(): pl.pallas_call(functools.partial(last_kernel, visits - 1, slots - 1), out...]
    pallas_call x1, Pallas kernels: 171 us -> 162 us  [body(): pl.pallas_call(functools.partial(kernel, n_wide, n_narrow, visits, slots,...]
    unnamed x4 -> x0, local copies, waits for them, and re-layouts: 4.55 us -> none
where the time goes in v3:
time: 198 us; the launch traced here: 196 us
  Pallas kernels  196 us (99%)
    pallas_call x1, Pallas kernels, body(): pl.pallas_call(functools.partial(kernel, n_wide, n_narrow, visits, slots,...  162 us
    pallas_call x1, Pallas kernels, body(): pl.pallas_call(functools.partial(last_kernel, visits - 1, slots - 1), out...  33.8 us

profile of v3, /device:TPU:15, one launch (start us, length us, event | category | flops | bytes accessed | tf_op | source)
XLA Modules:
  0.0 196.1 jit_solution(3319791319352754372)
XLA Ops:
  0.6 161.7 %sgd_sweep.1 = (f32[8,128,512]{2,1,0:T(8,128)}, f32[2,512,512]{2,1,0:T(8,128)}) custom-call(f32[8,128,512]{2,1,0:T(8,128)} %bitcast.5, f32[1,2,512,512]{3,2,1,0:T(8,128)} %items_ref.1, bf16[1,5,2,10,128,128]{5,4,3,2,1,0:T(8,128)(2,1)} %ratings_ref.3, s32[1,5,2,10]{3,2,1,0:T(2,128)} %rows_ref.3, s32[1,5,2,10]{3,2,1,0:T(2,128)} %cols_ref.3, s32[1,2,5]{2,1,0:T(2,128)} %bitcast.7), custom_call_target="tpu_custom_call" | custom-call | tf_op jit(solution)/shard_map/sgd_sweep/pallas_call | solution.py:334
  162.4 33.8 %last_slot.1 = (f32[8,128,512]{2,1,0:T(8,128)}, f32[1,2,4,128,512]{4,3,2,1,0:T(8,128)}) custom-call(f32[8,128,512]{2,1,0:T(8,128)} %get-tuple-element.6.users_ref, f32[2,4,128,512]{3,2,1,0:T(8,128)} %bitcast.6, bf16[1,5,2,10,128,128]{5,4,3,2,1,0:T(8,128)(2,1)} %ratings_ref.3, s32[1,5,2,10]{3,2,1,0:T(2,128)} %rows_ref.3, s32[1,5,2,10]{3,2,1,0:T(2,128)} %cols_ref.3, ...), custom_call_target="tpu_custom_call" | custom-call | tf_op jit(solution)/shard_map/last_slot/pallas_call | solution.py:360

commit v4 on v3

--- a/solution.py
+++ b/solution.py
@@ -15,7 +15,7 @@
 RELAY_ROWS = 128
 VMEM_GRANT = 56 << 20
 CHUNKS = 2
-CHUNK_ROWS = RELAY_ROWS // CHUNKS
+LAST_RELAY_ROWS = 96
 FORWARDS = ((0, 2, 0), (2, 2, 1), (4, 3, 0), (8, 3, 1))
 MESH = pl.DeviceIdType.MESH
 
@@ -93,7 +93,6 @@
     user_tiles = users_ref.shape[0]
     block_rows = items_ref.shape[2]
     item_tiles = block_rows // TILE
-    straight = block_rows - RELAY_ROWS
 
     w = lax.axis_index("wide")
     n = lax.axis_index("narrow")
@@ -108,19 +107,19 @@
     n_after = lax.rem(n + 1, n_narrow)
     n_before = lax.rem(n + n_narrow - 1, n_narrow)
 
-    loads = [
-        pltpu.make_async_copy(items_ref.at[0, 0], held.at[0], load_sem.at[0]),
-        pltpu.make_async_copy(users_ref, users.at[pl.ds(0, user_tiles)], load_sem.at[2]),
-        pltpu.make_async_copy(items_ref.at[0, 1], held.at[1], load_sem.at[1]),
-    ]
+    first = [pltpu.make_async_copy(items_ref.at[0, 0], held.at[0], load_sem.at[0])]
+    for i in range(user_tiles // 2):
+        two = pl.ds(2 * i, 2)
+        first.append(pltpu.make_async_copy(users_ref.at[two], users.at[two], load_sem.at[2 + i]))
+    second = pltpu.make_async_copy(items_ref.at[0, 1], held.at[1], load_sem.at[1])
 
     def rating_copy(t):
         return pltpu.make_async_copy(
             ratings_ref.at[0, t // slots, lax.rem(t, slots)], ratings.at[t], rating_sem.at[t]
         )
 
-    loads[0].start()
-    loads[1].start()
+    for copy in first:
+        copy.start()
     rating_copy(0).start()
     barrier = pltpu.get_barrier_semaphore()
     partners = [
@@ -152,25 +151,27 @@
     def ending_n(t):
         return jnp.where(t >= moves - slots, n_after, n)
 
-    def direct(t):
-        rows = pl.ds(0, straight)
+    def direct(t, relayed=RELAY_ROWS):
+        rows = pl.ds(0, block_rows - relayed)
         return remote(0, t, held.at[t, rows], held.at[t + slots, rows], (after, ending_n(t)))
 
-    def hop(number, chunk, t):
+    def hop(number, chunk, t, relayed=RELAY_ROWS):
         kind = 1 + (number - 1) * CHUNKS + chunk
-        rows = pl.ds(straight + chunk * CHUNK_ROWS, CHUNK_ROWS)
+        size = relayed // CHUNKS
+        rows = pl.ds(block_rows - relayed + chunk * size, size)
+        part = pl.ds(0, size)
         if number == 1:
-            src, dst, device = held.at[t, rows], relay_one.at[t, chunk], (down, n)
+            src, dst, device = held.at[t, rows], relay_one.at[t, chunk, part], (down, n)
         elif number == 2:
-            src, dst, device = relay_one.at[t, chunk], relay_two.at[t, chunk], (down, n)
+            src, dst, device = relay_one.at[t, chunk, part], relay_two.at[t, chunk, part], (down, n)
         else:
-            src, dst = relay_two.at[t, chunk], held.at[t + slots, rows]
+            src, dst = relay_two.at[t, chunk, part], held.at[t + slots, rows]
             device = (third_to, ending_n(t))
         return remote(kind, t, src, dst, device)
 
-    loads[0].wait()
-    loads[1].wait()
-    loads[2].start()
+    for copy in first:
+        copy.wait()
+    second.start()
     for t in range(1, moves + 1):
         rating_copy(t).start()
 
@@ -180,7 +181,7 @@
 
         @pl.when(t == 1)
         def _():
-            loads[2].wait()
+            second.wait()
 
         rating_copy(t).wait()
 
@@ -225,11 +226,16 @@
                 state = lax.fori_loop(done, position, one, state, unroll=2)
                 done = position
 
-            @pl.when((t >= 1) & (t <= moves))
+            @pl.when((t >= 1) & (t < moves))
             def _():
                 hop(number - 1, chunk, t - 1).wait_recv()
                 hop(number, chunk, t - 1).start()
 
+            @pl.when(t == moves)
+            def _():
+                hop(number - 1, chunk, moves - 1, LAST_RELAY_ROWS).wait_recv()
+                hop(number, chunk, moves - 1, LAST_RELAY_ROWS).start()
+
         if done < most:
             state = lax.fori_loop(done, most, one, state, unroll=2)
         user_at, item_at = state
@@ -237,11 +243,17 @@
         for i in range(item_tiles):
             held[t, i * TILE : (i + 1) * TILE, :] = work[item_at[i]]
 
-        @pl.when(t < moves)
+        @pl.when(t < moves - 1)
         def _():
             for chunk in range(CHUNKS):
                 hop(1, chunk, t).start()
             direct(t).start()
+
+        @pl.when(t == moves - 1)
+        def _():
+            for chunk in range(CHUNKS):
+                hop(1, chunk, moves - 1, LAST_RELAY_ROWS).start()
+            direct(moves - 1, LAST_RELAY_ROWS).start()
 
         for i in range(user_tiles):
             users[i] = users[user_at[i]]
@@ -257,9 +269,9 @@
     for copy in stores:
         copy.start()
 
-    direct(moves - 1).wait_recv()
+    direct(moves - 1, LAST_RELAY_ROWS).wait_recv()
     for chunk in range(CHUNKS):
-        hop(3, chunk, moves - 1).wait_recv()
+        hop(3, chunk, moves - 1, LAST_RELAY_ROWS).wait_recv()
     last = pltpu.make_async_copy(held.at[moves + 1], blocks_out.at[1], load_sem.at[1])
     last.start()
 
@@ -270,7 +282,11 @@
                 hop(number, chunk, t).wait_send()
         return carry
 
-    lax.fori_loop(0, moves, drain, 0)
+    lax.fori_loop(0, moves - 1, drain, 0)
+    direct(moves - 1, LAST_RELAY_ROWS).wait_send()
+    for number in (1, 2, 3):
+        for chunk in range(CHUNKS):
+            hop(number, chunk, moves - 1, LAST_RELAY_ROWS).wait_send()
     for copy in stores:
         copy.wait()
     last.wait()
@@ -289,32 +305,76 @@
     items_out,
     users,
     items,
+    others,
     ratings,
     sems,
+    user_sems,
+    item_sems,
 ):
-    users_in = pltpu.make_async_copy(users_ref, users, sems.at[0])
-    items_in = pltpu.make_async_copy(blocks_ref.at[slot], items, sems.at[1])
-    ratings_in = pltpu.make_async_copy(ratings_ref.at[0, visit, slot], ratings, sems.at[2])
-    rest = pltpu.make_async_copy(blocks_ref.at[0], items_out.at[0, 0], sems.at[3])
-    for copy in (users_in, items_in, ratings_in, rest):
+    user_tiles, item_tiles = users.shape[0], items.shape[0]
+    most = ratings.shape[0]
+    pieces = user_tiles // 2
+    copies = [
+        pltpu.make_async_copy(blocks_ref.at[slot], items, sems.at[0]),
+        pltpu.make_async_copy(ratings_ref.at[0, visit, slot], ratings, sems.at[1]),
+    ]
+    for i in range(pieces):
+        two = pl.ds(2 * i, 2)
+        copies.append(pltpu.make_async_copy(users_ref.at[two], users.at[two], sems.at[3 + i]))
+    rest_in = pltpu.make_async_copy(blocks_ref.at[0], others, sems.at[2])
+    for copy in copies:
         copy.start()
-    for copy in (users_in, items_in, ratings_in):
+    rest_in.start()
+
+    def user_back(i):
+        return pltpu.make_async_copy(users.at[i], users_out.at[i], user_sems.at[i])
+
+    def item_back(i):
+        return pltpu.make_async_copy(items.at[i], items_out.at[0, slot, i], item_sems.at[i])
+
+    count = count_ref[0, slot, visit]
+
+    def later(table, index, start):
+        found = jnp.int32(0)
+        for k in range(most):
+            same = (table[0, visit, slot, k] == index) & (k < count) & (k >= start)
+            found = jnp.where(same, 1, found)
+        return found == 1
+
+    for copy in copies:
         copy.wait()
+    for table, tiles, back in ((rows_ref, user_tiles, user_back), (cols_ref, item_tiles, item_back)):
+        for i in range(tiles):
+
+            @pl.when(jnp.logical_not(later(table, i, 0)))
+            def _():
+                back(i).start()
+
+    rest_in.wait()
+    rest_back = pltpu.make_async_copy(others, items_out.at[0, 0], sems.at[2])
+    rest_back.start()
 
     def one(k, carry):
         a, c = rows_ref[0, visit, slot, k], cols_ref[0, visit, slot, k]
         users[a], items[c] = tile_update(users[a], items[c], ratings[k])
+
+        @pl.when(jnp.logical_not(later(rows_ref, a, k + 1)))
+        def _():
+            user_back(a).start()
+
+        @pl.when(jnp.logical_not(later(cols_ref, c, k + 1)))
+        def _():
+            item_back(c).start()
+
         return carry
 
-    lax.fori_loop(0, count_ref[0, slot, visit], one, 0)
-
-    users_back = pltpu.make_async_copy(users, users_out, sems.at[0])
-    items_back = pltpu.make_async_copy(items, items_out.at[0, slot], sems.at[1])
-    users_back.start()
-    items_back.start()
-    rest.wait()
-    users_back.wait()
-    items_back.wait()
+    lax.fori_loop(0, count, one, 0)
+
+    rest_back.wait()
+    for i in range(user_tiles):
+        user_back(i).wait()
+    for i in range(item_tiles):
+        item_back(i).wait()
 
 
 def body(n_wide, n_narrow, user_factors, item_factors, tile_rows, tile_cols, tile_count, ratings):
@@ -331,6 +391,7 @@
     f32 = jnp.float32
     tables = (tile_rows, tile_cols, tile_count.swapaxes(1, 2))
     shape = jax.ShapeDtypeStruct
+    item_tiles = block_rows // TILE
     users_then, blocks_then = pl.pallas_call(
         functools.partial(kernel, n_wide, n_narrow, visits, slots, most),
         out_shape=(
@@ -343,10 +404,10 @@
             pltpu.VMEM((user_tiles + most, TILE, rank), f32),
             pltpu.VMEM((block_rows // TILE + most, TILE, rank), f32),
             pltpu.VMEM((steps, block_rows, rank), f32),
-            pltpu.VMEM((moves, CHUNKS, CHUNK_ROWS, rank), f32),
-            pltpu.VMEM((moves, CHUNKS, CHUNK_ROWS, rank), f32),
+            pltpu.VMEM((moves, CHUNKS, RELAY_ROWS // CHUNKS, rank), f32),
+            pltpu.VMEM((moves, CHUNKS, RELAY_ROWS // CHUNKS, rank), f32),
             pltpu.VMEM((moves + 1, most, TILE, TILE), ratings.dtype),
-            pltpu.SemaphoreType.DMA((3,)),
+            pltpu.SemaphoreType.DMA((2 + user_tiles // 2,)),
             pltpu.SemaphoreType.DMA((moves + 1,)),
             pltpu.SemaphoreType.DMA((1 + 3 * CHUNKS, moves)),
             pltpu.SemaphoreType.DMA((1 + 3 * CHUNKS, moves)),
@@ -356,7 +417,6 @@
         ),
         name="sgd_sweep",
     )(user_blocks, item_factors, ratings, *tables)
-    item_tiles = block_rows // TILE
     users_new, items_new = pl.pallas_call(
         functools.partial(last_kernel, visits - 1, slots - 1),
         out_shape=(
@@ -368,8 +428,11 @@
         scratch_shapes=[
             pltpu.VMEM(user_blocks.shape, f32),
             pltpu.VMEM((item_tiles, TILE, rank), f32),
+            pltpu.VMEM((item_tiles, TILE, rank), f32),
             pltpu.VMEM((most, TILE, TILE), ratings.dtype),
-            pltpu.SemaphoreType.DMA((4,)),
+            pltpu.SemaphoreType.DMA((3 + user_tiles // 2,)),
+            pltpu.SemaphoreType.DMA((user_tiles,)),
+            pltpu.SemaphoreType.DMA((item_tiles,)),
         ],
         compiler_params=pltpu.CompilerParams(vmem_limit_bytes=VMEM_GRANT),
         name="last_slot",

time: 198 us -> 168 us (0.85)
  Pallas kernels: 196 us -> 167 us
    pallas_call x1, Pallas kernels: 33.8 us -> 6.38 us  [body(): pl.pallas_call(functools.partial(last_kernel, visits - 1, slots - 1), out...]
where the time goes in v4:
time: 168 us
  Pallas kernels  167 us (99%)
    pallas_call x1, Pallas kernels, body(): pl.pallas_call(functools.partial(kernel, n_wide, n_narrow, visits, slots,...  161 us
    pallas_call x1, Pallas kernels, body(): pl.pallas_call(functools.partial(last_kernel, visits - 1, slots - 1), out...  6.38 us

profile of v4, /device:TPU:15, one launch (start us, length us, event | category | flops | bytes accessed | tf_op | source)
XLA Modules:
  0.0 167.7 jit_solution(7596643270747613124)
XLA Ops:
  0.6 160.7 %sgd_sweep.1 = (f32[8,128,512]{2,1,0:T(8,128)}, f32[2,512,512]{2,1,0:T(8,128)}) custom-call(f32[8,128,512]{2,1,0:T(8,128)} %bitcast.5, f32[1,2,512,512]{3,2,1,0:T(8,128)} %items_ref.1, bf16[1,5,2,10,128,128]{5,4,3,2,1,0:T(8,128)(2,1)} %ratings_ref.3, s32[1,5,2,10]{3,2,1,0:T(2,128)} %rows_ref.3, s32[1,5,2,10]{3,2,1,0:T(2,128)} %cols_ref.3, s32[1,2,5]{2,1,0:T(2,128)} %bitcast.7), custom_call_target="tpu_custom_call" | custom-call | tf_op jit(solution)/shard_map/sgd_sweep/pallas_call | solution.py:395
  161.3 6.4 %last_slot.1 = (f32[8,128,512]{2,1,0:T(8,128)}, f32[1,2,4,128,512]{4,3,2,1,0:T(8,128)}) custom-call(f32[8,128,512]{2,1,0:T(8,128)} %get-tuple-element.6.users_ref, f32[2,4,128,512]{3,2,1,0:T(8,128)} %bitcast.6, bf16[1,5,2,10,128,128]{5,4,3,2,1,0:T(8,128)(2,1)} %ratings_ref.3, s32[1,5,2,10]{3,2,1,0:T(2,128)} %rows_ref.3, s32[1,5,2,10]{3,2,1,0:T(2,128)} %cols_ref.3, ...), custom_call_target="tpu_custom_call" | custom-call | tf_op jit(solution)/shard_map/last_slot/pallas_call | solution.py:420

commit v5 on v4

--- a/solution.py
+++ b/solution.py
@@ -269,12 +269,6 @@
     for copy in stores:
         copy.start()
 
-    direct(moves - 1, LAST_RELAY_ROWS).wait_recv()
-    for chunk in range(CHUNKS):
-        hop(3, chunk, moves - 1, LAST_RELAY_ROWS).wait_recv()
-    last = pltpu.make_async_copy(held.at[moves + 1], blocks_out.at[1], load_sem.at[1])
-    last.start()
-
     def drain(t, carry):
         direct(t).wait_send()
         for number in (1, 2, 3):
@@ -283,12 +277,18 @@
         return carry
 
     lax.fori_loop(0, moves - 1, drain, 0)
+    for copy in stores:
+        copy.wait()
+
+    direct(moves - 1, LAST_RELAY_ROWS).wait_recv()
+    for chunk in range(CHUNKS):
+        hop(3, chunk, moves - 1, LAST_RELAY_ROWS).wait_recv()
+    last = pltpu.make_async_copy(held.at[moves + 1], blocks_out.at[1], load_sem.at[1])
+    last.start()
     direct(moves - 1, LAST_RELAY_ROWS).wait_send()
     for number in (1, 2, 3):
         for chunk in range(CHUNKS):
             hop(number, chunk, moves - 1, LAST_RELAY_ROWS).wait_send()
-    for copy in stores:
-        copy.wait()
     last.wait()
 
 

time: 168 us -> 171 us (1.018)
  Pallas kernels: 167 us -> 171 us
    pallas_call x1, Pallas kernels: 6.38 us -> 9.93 us  [body(): pl.pallas_call(functools.partial(last_kernel, visits - 1, slots - 1), out...]
where the time goes in v5:
time: 171 us
  Pallas kernels  171 us (100%)
    pallas_call x1, Pallas kernels, body(): pl.pallas_call(functools.partial(kernel, n_wide, n_narrow, visits, slots,...  161 us
    pallas_call x1, Pallas kernels, body(): pl.pallas_call(functools.partial(last_kernel, visits - 1, slots - 1), out...  9.93 us

profile of v5, /device:TPU:15, one launch (start us, length us, event | category | flops | bytes accessed | tf_op | source)
XLA Modules:
  0.0 171.2 jit_solution(18241202961440668155)
XLA Ops:
  0.6 160.7 %sgd_sweep.1 = (f32[8,128,512]{2,1,0:T(8,128)}, f32[2,512,512]{2,1,0:T(8,128)}) custom-call(f32[8,128,512]{2,1,0:T(8,128)} %bitcast.5, f32[1,2,512,512]{3,2,1,0:T(8,128)} %items_ref.1, bf16[1,5,2,10,128,128]{5,4,3,2,1,0:T(8,128)(2,1)} %ratings_ref.3, s32[1,5,2,10]{3,2,1,0:T(2,128)} %rows_ref.3, s32[1,5,2,10]{3,2,1,0:T(2,128)} %cols_ref.3, s32[1,2,5]{2,1,0:T(2,128)} %bitcast.7), custom_call_target="tpu_custom_call" | custom-call | tf_op jit(solution)/shard_map/sgd_sweep/pallas_call | solution.py:395
  161.3 9.9 %last_slot.1 = (f32[8,128,512]{2,1,0:T(8,128)}, f32[1,2,4,128,512]{4,3,2,1,0:T(8,128)}) custom-call(f32[8,128,512]{2,1,0:T(8,128)} %get-tuple-element.6.users_ref, f32[2,4,128,512]{3,2,1,0:T(8,128)} %bitcast.6, bf16[1,5,2,10,128,128]{5,4,3,2,1,0:T(8,128)(2,1)} %ratings_ref.3, s32[1,5,2,10]{3,2,1,0:T(2,128)} %rows_ref.3, s32[1,5,2,10]{3,2,1,0:T(2,128)} %cols_ref.3, ...), custom_call_target="tpu_custom_call" | custom-call | tf_op jit(solution)/shard_map/last_slot/pallas_call | solution.py:420

commit v6 on v5

--- a/solution.py
+++ b/solution.py
@@ -13,7 +13,7 @@
 RING = 4
 TILE = 128
 RELAY_ROWS = 128
-VMEM_GRANT = 56 << 20
+VMEM_GRANT = 48 << 20
 CHUNKS = 2
 LAST_RELAY_ROWS = 96
 FORWARDS = ((0, 2, 0), (2, 2, 1), (4, 3, 0), (8, 3, 1))

time: 171 us -> 170 us (level); the launches traced: 171 us -> 168 us
  Pallas kernels: 171 us -> 165 us
  local copies, waits for them, and re-layouts: 0 us -> 2.05 us
    pallas_call x1, Pallas kernels: 9.93 us -> 5.62 us  [body(): pl.pallas_call(functools.partial(last_kernel, visits - 1, slots - 1), out...]
    unnamed x0 -> x6, local copies, waits for them, and re-layouts: none -> 2.05 us
where the time goes in v6:
time: 170 us; the launch traced here: 168 us
  Pallas kernels  165 us (97%)
  local copies, waits for them, and re-layouts  2.05 us (1%)
    pallas_call x1, Pallas kernels, body(): pl.pallas_call(functools.partial(kernel, n_wide, n_narrow, visits, slots,...  159 us
    pallas_call x1, Pallas kernels, body(): pl.pallas_call(functools.partial(last_kernel, visits - 1, slots - 1), out...  5.62 us

profile of v6, /device:TPU:15, one launch (start us, length us, event | category | flops | bytes accessed | tf_op | source)
XLA Modules:
  0.0 167.7 jit_solution(13395414283420084298)
XLA Ops:
  0.6 0.0 copy-start
  0.6 0.7 copy-done
  1.3 0.0 copy-start.1
  1.3 0.7 copy-done.1
  2.0 0.0 copy-start.2
  2.0 0.7 copy-done.2
  2.7 159.4 %sgd_sweep.1 = (f32[8,128,512]{2,1,0:T(8,128)S(1)}, f32[2,512,512]{2,1,0:T(8,128)S(1)}) custom-call(f32[8,128,512]{2,1,0:T(8,128)} %bitcast.8, f32[1,2,512,512]{3,2,1,0:T(8,128)} %items_ref.1, bf16[1,5,2,10,128,128]{5,4,3,2,1,0:T(8,128)(2,1)} %ratings_ref.3, s32[1,5,2,10]{3,2,1,0:T(2,128)S(1)} %copy-done, s32[1,5,2,10]{3,2,1,0:T(2,128)S(1)} %copy-done.1, ...), custom_call_target="tpu_custom_call" | custom-call | tf_op jit(solution)/shard_map/sgd_sweep/pallas_call | solution.py:395
  162.1 5.6 %last_slot.1 = (f32[8,128,512]{2,1,0:T(8,128)}, f32[1,2,4,128,512]{4,3,2,1,0:T(8,128)}) custom-call(f32[8,128,512]{2,1,0:T(8,128)S(1)} %get-tuple-element.6.users_ref, f32[2,4,128,512]{3,2,1,0:T(8,128)S(1)} %bitcast.5, bf16[1,5,2,10,128,128]{5,4,3,2,1,0:T(8,128)(2,1)} %ratings_ref.3, s32[1,5,2,10]{3,2,1,0:T(2,128)S(1)} %copy-done, ...), custom_call_target="tpu_custom_call" | custom-call | tf_op jit(solution)/shard_map/last_slot/pallas_call | solution.py:420
Async XLA Ops:
  0.6 0.7 copy-start
  1.3 0.7 copy-start.1
  2.0 0.7 copy-start.2
